TPU v7x, 32 devices: a whole 2x2x4 slice. The times are simulated.
32 devices in a mesh: dp: 8 (over y, x, core), space: 4 (over z).
Axes of the slice: x: 2, y: 2, z: 4, core: 2. Of those that a mesh axis runs over, the one named last changes fastest.
Arguments:
- inputs: bfloat16 [8, 48, 128, 768], P('dp', 'space'), may hold values from -6 to 6
- gain: float32 [768], replicated, may hold values from 0.1 to 1.9
- w_in: bfloat16 [2, 768, 96], P(None, 'space'), may hold values from -0.4375 to 0.4375
- b_in: float32 [2, 768], P(None, 'space'), may hold values from -3 to 3
- w_out: bfloat16 [2, 768, 96], P(None, 'space'), may hold values from -0.4375 to 0.4375
- d_out: bfloat16 [8, 48, 128, 768], P('dp', 'space'), may hold values from -6 to 6
Outputs:
- d_inputs: bfloat16 [8, 48, 128, 768], P('dp', 'space')
- d_w_in: float32 [2, 768, 96], P(None, 'space')
- d_b_in: float32 [2, 768], P(None, 'space')
- d_w_out: float32 [2, 768, 96], P(None, 'space')
- d_gain: float32 [768], replicated
All inputs are finite; a program needn't handle non-finite values.
Results may differ from a plain program's by a relative error of at most 0.012.
Values may be sent and summed in bfloat16 or wider, within the bound.
A program may use at most 128 MiB of HBM per device.

v0:
```python
import math

import jax
import jax.numpy as jnp
from jax import lax
from jax.sharding import PartitionSpec as P

norm_eps = 1e-05
root_coef = math.sqrt(2.0 / math.pi)
cubic_coef = 0.044715


def dft_tables(length, kept):
    index_rows = jnp.arange(length, dtype=jnp.int32)
    index_cols = jnp.arange(kept, dtype=jnp.int32)
    product = index_rows[:, None] * index_cols[None, :] % length
    angles = 2.0 * math.pi / length * product.astype(jnp.float32)
    scale = 1.0 / math.sqrt(length)
    return (jnp.cos(angles) * scale, jnp.sin(angles) * scale)


def half_signs(kept):
    return jnp.concatenate([jnp.ones((kept,), jnp.float32), -jnp.ones((kept,), jnp.float32)])


def swap_parts(values, signs):
    return jnp.roll(values, values.shape[-1] // 2, axis=-1) * signs.astype(values.dtype)


def rows_apply(spectra, row_tables, signs):
    paired = jnp.einsum("tgh,shcm->tsgcm", row_tables, spectra, preferred_element_type=jnp.float32)
    return paired[0] + swap_parts(paired[1], signs)


def block_apply(values, weights, signs):
    real_part = jnp.einsum(
        "sgbim,bio->sgbom", values, weights[0], preferred_element_type=jnp.float32
    )
    imag_part = jnp.einsum(
        "sgbim,bio->sgbom", values, weights[1], preferred_element_type=jnp.float32
    )
    return real_part + swap_parts(imag_part, signs)


def block_adjoint(values, weights, signs):
    real_part = jnp.einsum(
        "sgbom,bio->sgbim", values, weights[0], preferred_element_type=jnp.float32
    )
    imag_part = jnp.einsum(
        "sgbom,bio->sgbim", values, weights[1], preferred_element_type=jnp.float32
    )
    return real_part + swap_parts(imag_part, signs)


def block_weight_grad(inputs_spec, grads_spec, signs):
    real_part = jnp.einsum(
        "sgbim,sgbom->bio", inputs_spec, grads_spec, preferred_element_type=jnp.float32
    )
    imag_part = jnp.einsum(
        "sgbim,sgbom->bio",
        swap_parts(inputs_spec, signs),
        grads_spec,
        preferred_element_type=jnp.float32,
    )
    return jnp.stack([real_part, imag_part])


def gelu_value(values):
    inner = root_coef * (values + cubic_coef * values * values * values)
    return 0.5 * values * (1.0 + jnp.tanh(inner))


def gelu_slope(values):
    inner = root_coef * (values + cubic_coef * values * values * values)
    tangent = jnp.tanh(inner)
    return 0.5 * (1.0 + tangent) + 0.5 * values * (1.0 - tangent * tangent) * root_coef * (
        1.0 + 3.0 * cubic_coef * values * values
    )


def on_device(inputs, gain, w_in, b_in, w_out, d_out):
    samples, rows, width, channels = inputs.shape
    kept = width // 2
    height = rows * lax.axis_size("space")
    local_channels = w_in.shape[1]
    block = w_in.shape[2]
    groups = local_channels // block
    cos_rows, sin_rows = dft_tables(height, height)
    row_tables = jnp.stack([cos_rows, sin_rows]).astype(jnp.bfloat16)
    cos_cols, sin_cols = dft_tables(width, kept)
    forward_cols = jnp.concatenate([cos_cols, -sin_cols], axis=1).astype(jnp.bfloat16)
    doubling = jnp.where(jnp.arange(kept, dtype=jnp.int32) == 0, 1.0, 2.0).astype(jnp.float32)
    inverse_cols = jnp.concatenate([cos_cols * doubling, -sin_cols * doubling], axis=1).astype(
        jnp.bfloat16
    )
    plus_minus = half_signs(kept)
    minus_plus = -plus_minus
    weights_in = w_in.reshape(2, groups, block, block)
    weights_out = w_out.reshape(2, groups, block, block)
    bias_parts = b_in.reshape(2, groups, block)
    bias_full = jnp.concatenate(
        [
            jnp.broadcast_to(bias_parts[0][:, :, None], (groups, block, kept)),
            jnp.broadcast_to(bias_parts[1][:, :, None], (groups, block, kept)),
        ],
        axis=-1,
    )
    values = inputs.astype(jnp.float32)
    centre = jnp.mean(values, axis=-1, keepdims=True)
    mean_removed = values - centre
    variance = jnp.mean(mean_removed * mean_removed, axis=-1, keepdims=True)
    reciprocal_scale = lax.rsqrt(variance + norm_eps)
    standardized_input = mean_removed * reciprocal_scale
    normalized_input = (standardized_input * gain).astype(jnp.bfloat16)
    spectrum_cols = jnp.einsum(
        "srwc,wm->srcm", normalized_input, forward_cols, preferred_element_type=jnp.float32
    ).astype(jnp.bfloat16)
    spectrum_full = lax.all_to_all(spectrum_cols, "space", split_axis=2, concat_axis=1, tiled=True)
    modes = rows_apply(spectrum_full, row_tables, plus_minus).astype(jnp.bfloat16)
    modes = modes.reshape(samples, height, groups, block, width)
    preact = block_apply(modes, weights_in, minus_plus) + bias_full
    hidden = gelu_value(preact).astype(jnp.bfloat16)
    grad_cols = jnp.einsum(
        "srwc,wm->srcm", d_out, inverse_cols, preferred_element_type=jnp.float32
    ).astype(jnp.bfloat16)
    grad_full = lax.all_to_all(grad_cols, "space", split_axis=2, concat_axis=1, tiled=True)
    grad_out = rows_apply(grad_full, row_tables, plus_minus).astype(jnp.bfloat16)
    grad_out = grad_out.reshape(samples, height, groups, block, width)
    grad_w_out = block_weight_grad(hidden, grad_out, minus_plus)
    d_hidden = block_adjoint(grad_out, weights_out, plus_minus)
    d_preact = (d_hidden * gelu_slope(preact)).astype(jnp.bfloat16)
    grad_w_in = block_weight_grad(modes, d_preact, minus_plus)
    bias_sums = jnp.sum(
        d_preact.reshape(samples, height, groups, block, 2, kept), axis=(0, 1, 5), dtype=jnp.float32
    )
    grad_b_in = jnp.moveaxis(bias_sums, 2, 0).reshape(2, local_channels)
    d_modes = block_adjoint(d_preact, weights_in, plus_minus).astype(jnp.bfloat16)
    d_modes = d_modes.reshape(samples, height, local_channels, width)
    d_spectrum = rows_apply(d_modes, row_tables, minus_plus).astype(jnp.bfloat16)
    d_cols = lax.all_to_all(d_spectrum, "space", split_axis=1, concat_axis=2, tiled=True)
    d_filter = jnp.einsum("srcm,wm->srwc", d_cols, forward_cols, preferred_element_type=jnp.float32)
    normalized_gradient = d_out.astype(jnp.float32) + d_filter
    gain_component = jnp.sum(normalized_gradient * standardized_input, axis=(0, 1, 2))
    rescaled_output = normalized_gradient * gain
    value_gradient = reciprocal_scale * (
        rescaled_output
        - jnp.mean(rescaled_output, axis=-1, keepdims=True)
        - standardized_input
        * jnp.mean(rescaled_output * standardized_input, axis=-1, keepdims=True)
    )
    d_inputs = value_gradient.astype(jnp.bfloat16)
    flat_w_in = grad_w_in.reshape(2, local_channels, block)
    flat_w_out = grad_w_out.reshape(2, local_channels, block)
    sum_w_in, sum_b_in, sum_w_out = lax.psum((flat_w_in, grad_b_in, flat_w_out), "dp")
    sum_gain = lax.psum(gain_component, ("dp", "space"))
    return (d_inputs, sum_w_in, sum_b_in, sum_w_out, sum_gain)


def solution(mesh):
    return jax.shard_map(
        on_device,
        mesh=mesh,
        in_specs=(
            P("dp", "space", None, None),
            P(),
            P(None, "space", None),
            P(None, "space"),
            P(None, "space", None),
            P("dp", "space", None, None),
        ),
        out_specs=(
            P("dp", "space", None, None),
            P(None, "space", None),
            P(None, "space"),
            P(None, "space", None),
            P(),
        ),
        check_vma=False,
    )
```

profile of v0, /device:TPU:0, one launch (start us, length us, event | category | flops | bytes accessed | tf_op | source)
XLA Modules:
  0.0 366.8 jit_solution(1452528982835782967)
XLA Ops:
  7.3 3.8 %convert_bitcast_fusion.1 = bf16[1,12,768,128]{2,3,1,0:T(8,128)(2,1)} fusion(bf16[1,12,128,768]{3,2,1,0:T(8,128)(2,1)} %param.11, bf16[128,64]{0,1:T(8,128)(2,1)S(1)} %get-tuple-element.43, bf16[128,64]{0,1:T(8,128)(2,1)S(1)} %get-tuple-element.44), kind=kOutput, calls=%fused_computation.85 | convolution fusion | flops 303235072 | bytes 4751360 | tf_op jit(solution)/shard_map/srwc,wm->srcm/dot_general | solution.py:123
  11.2 5.1 %copy.82 = bf16[1,12,768,128]{3,1,0,2:T(8,128)(2,1)} copy(bf16[1,12,768,128]{2,3,1,0:T(8,128)(2,1)} %convert_bitcast_fusion.1) | data formatting | bytes 4718592 | tf_op jit(solution)/shard_map/convert_element_type | solution.py:125
  16.3 6.4 %all-to-all-start = ((bf16[1,12,768,128]{3,1,0,2:T(8,128)(2,1)}), bf16[1,12,768,128]{3,1,0,2:T(8,128)(2,1)}, u32[]{:S(2)}, u32[]{:S(2)}) async-start(bf16[1,12,768,128]{3,1,0,2:T(8,128)(2,1)} %copy.82), calls=%async_computation | async-start | bytes 6291456 | tf_op jit(solution)/shard_map/all_to_all | solution.py:126
  22.9 0.4 convert_reduce_fusion
  23.3 0.8 fusion.12
  24.2 1.7 convert_bitcast_fusion
  25.9 3.3 copy.91
  29.2 64.4 %all-to-all-done = bf16[1,12,768,128]{3,1,0,2:T(8,128)(2,1)} async-done(((bf16[1,12,768,128]{3,1,0,2:T(8,128)(2,1)}), bf16[1,12,768,128]{3,1,0,2:T(8,128)(2,1)}, u32[]{:S(2)}, u32[]{:S(2)}) %all-to-all-start) | async-done | bytes 2359328 | tf_op jit(solution)/shard_map/all_to_all | solution.py:126
  93.6 4.2 %all-to-all-start.1 = ((bf16[1,12,768,128]{3,1,0,2:T(8,128)(2,1)}), bf16[1,12,768,128]{3,1,0,2:T(8,128)(2,1)S(1)}, u32[]{:S(2)}, u32[]{:S(2)}) async-start(bf16[1,12,768,128]{3,1,0,2:T(8,128)(2,1)} %copy.91), calls=%async_computation.1 | async-start | bytes 6291456 | tf_op jit(solution)/shard_map/all_to_all | solution.py:118
  98.4 0.8 fusion.101
  99.3 2.5 copy.83
  101.8 1.6 copy.84
  103.4 64.0 %all-to-all-done.1 = bf16[1,12,768,128]{3,1,0,2:T(8,128)(2,1)S(1)} async-done(((bf16[1,12,768,128]{3,1,0,2:T(8,128)(2,1)}), bf16[1,12,768,128]{3,1,0,2:T(8,128)(2,1)S(1)}, u32[]{:S(2)}, u32[]{:S(2)}) %all-to-all-start.1) | async-done | bytes 2359328 | tf_op jit(solution)/shard_map/all_to_all | solution.py:118
  167.3 0.6 copy.92
  168.1 1.7 convolution_bitcast_fusion.1
  169.8 0.7 fusion.94
  170.6 1.5 fusion.100
  172.1 4.2 %copy.96 = f32[48,2,96,64]{3,2,0,1:T(8,128)} copy(f32[48,2,96,64]{3,0,2,1:T(8,128)S(1)} %bitcast.216) | data formatting | bytes 4718592 | tf_op jit(solution)/shard_map/jit(_roll_static)/concatenate | solution.py:27
  176.4 0.8 copy-done.1
  177.2 3.6 copy.95
  180.8 1.7 convolution_bitcast_fusion.2
  182.5 2.9 fusion.93
  185.3 3.9 %fusion.98 = (f32[1,48,192,64]{3,1,2,0:T(8,128)}, f32[1,48,192,64]{3,1,2,0:T(8,128)S(1)}) fusion(f32[1,48,192,128]{3,1,2,0:T(8,128)S(1)} %get-tuple-element.13), kind=kLoop, calls=%fused_computation.147 | loop fusion | bytes 9437184 | tf_op jit(solution)/shard_map/jit(_roll_static)/slice | solution.py:27
  189.2 6.0 %copy.86 = f32[48,2,96,64]{3,2,0,1:T(8,128)} copy(f32[48,2,96,64]{3,0,2,1:T(8,128)} %bitcast.224) | data formatting | bytes 4718592 | tf_op jit(solution)/shard_map/jit(_roll_static)/concatenate | solution.py:27
  195.2 3.6 copy.87
  198.9 8.7 %fusion.23 = (bf16[48,2,96,128]{3,2,0,1:T(8,128)(2,1)S(1)}, bf16[48,2,96,128]{3,2,0,1:T(8,128)(2,1)S(1)}) fusion(f32[48,2,96,64]{3,2,0,1:T(8,128)} %copy.87, f32[48,2,96,64]{3,2,0,1:T(8,128)} %copy.86, f32[48,2,96,128]{3,0,2,1:T(8,128)} %bitcast.220, f32[128]{0:T(128)S(1)} %copy-done.15, f32[48,2,96,64]{3,2,0,1:T(8,128)S(1)} %bitcast.219, ...), kind=kLoop, calls=%fused_computation.32 | loop fusion | flops 9437184 | bytes 23593472 | tf_op jit(solution)/shard_map/convert_element_type | solution.py:127
  207.6 0.8 convolution_bitcast_fusion.4
  208.4 3.8 %fusion.99 = (f32[1,48,2,96,64]{4,3,1,2,0:T(8,128)S(1)}, f32[1,48,2,96,64]{4,3,1,2,0:T(8,128)}) fusion(f32[1,48,2,96,128]{4,3,1,2,0:T(8,128)S(1)} %convolution_bitcast_fusion.4), kind=kLoop, calls=%fused_computation.148 | loop fusion | bytes 9437184 | tf_op jit(solution)/shard_map/jit(_roll_static)/slice | solution.py:27
  212.2 0.8 convolution_bitcast_fusion.3
  213.0 5.3 %fusion.97 = (f32[1,48,2,96,64]{4,3,1,2,0:T(8,128)}, f32[1,48,2,96,64]{4,3,1,2,0:T(8,128)}) fusion(f32[1,48,2,96,128]{4,3,1,2,0:T(8,128)S(1)} %convolution_bitcast_fusion.3), kind=kLoop, calls=%fused_computation.146 | loop fusion | bytes 9437184 | tf_op jit(solution)/shard_map/jit(_roll_static)/slice | solution.py:27
  218.3 6.0 %multiply_convert_fusion = (bf16[1,48,2,96,128]{4,3,1,2,0:T(8,128)(2,1)}, f32[1,48,2,96,128]{4,3,1,2,0:T(8,128)S(1)}) fusion(f32[2,96,128]{2,1,0:T(8,128)S(1)} %pad_maximum_fusion.2, f32[128]{0:T(128)S(1)} %copy-done.16, f32[1,48,2,96,64]{4,3,1,2,0:T(8,128)} %get-tuple-element.25, f32[1,48,2,96,64]{4,3,1,2,0:T(8,128)S(1)} %get-tuple-element.24, ...), kind=kOutput, calls=%fused_computation.49 | convolution fusion | flops 241827840 | bytes 14291456 | tf_op jit(solution)/shard_map/sgbim,bio->sgbom/dot_general | solution.py:36
  224.3 4.9 %convert_reduce_fusion.1 = (f32[2,96,128]{2,1,0:T(8,128)S(1)}, bf16[1,48,2,96,128]{4,3,1,2,0:T(8,128)(2,1)S(1)}) fusion(f32[1,48,2,96,128]{4,3,1,2,0:T(8,128)S(1)} %get-tuple-element.40, f32[128]{0:T(128)S(1)} %copy-done.15, f32[1,48,2,96,64]{4,3,1,2,0:T(8,128)S(1)} %copy-done.12, f32[1,48,2,96,64]{4,3,1,2,0:T(8,128)S(1)} %copy-done.11, ...), kind=kOutput, calls=%fused_computation.50 | convolution fusion | flops 254779392 | bytes 14291456 | tf_op jit(solution)/shard_map/sgbom,bio->sgbim/dot_general | solution.py:46
  229.3 0.8 fusion.59
  230.0 3.8 %fusion.96 = (f32[1,48,2,96,64]{4,3,1,2,0:T(8,128)S(1)}, f32[1,48,2,96,64]{4,3,1,2,0:T(8,128)}) fusion(f32[1,48,2,96,128]{4,3,1,2,0:T(8,128)S(1)} %fusion.59), kind=kLoop, calls=%fused_computation.145 | loop fusion | bytes 9437184 | tf_op jit(solution)/shard_map/jit(_roll_static)/slice | solution.py:27
  233.8 3.9 %fusion.30 = bf16[1,48,2,96,128]{4,3,1,2,0:T(8,128)(2,1)S(1)} fusion(f32[1,48,2,96,64]{4,3,1,2,0:T(8,128)} %get-tuple-element.19, f32[1,48,2,96,64]{4,3,1,2,0:T(8,128)S(1)} %get-tuple-element.18, f32[128]{0:T(128)S(1)} %copy-done.15, bf16[2,96,96,1]{2,1,3,0:T(8,128)(2,1)S(1)} %bitcast.234, bf16[1,48,2,96,128]{4,3,1,2,0:T(8,128)(2,1)S(1)} %get-tuple-element.42), kind=kOutput, calls=%fused_computation.43 | convolution fusion | flops 231211008 | bytes 9474560 | tf_op jit(solution)/shard_map/sgbom,bio->sgbim/dot_general | solution.py:46
  237.7 0.3 copy.100
  238.1 1.7 convolution_bitcast_fusion
  239.8 0.4 slice_bitcast_fusion
  240.2 5.1 %fusion.95 = (f32[1,48,192,64]{3,1,2,0:T(8,128)}, f32[1,48,192,64]{3,1,2,0:T(8,128)}) fusion(f32[1,48,192,128]{3,1,2,0:T(8,128)S(1)} %slice_bitcast_fusion), kind=kLoop, calls=%fused_computation.144 | loop fusion | bytes 9437184 | tf_op jit(solution)/shard_map/jit(_roll_static)/slice | solution.py:27
  245.3 5.3 %fusion.21 = bf16[1,48,192,128]{3,1,2,0:T(8,128)(2,1)S(1)} fusion(f32[2,1,48,192,128]{4,2,0,3,1:T(8,128)S(1)} %convolution_bitcast_fusion, f32[1,48,192,64]{3,1,2,0:T(8,128)} %get-tuple-element.17, f32[1,48,192,64]{3,1,2,0:T(8,128)} %get-tuple-element.16, f32[128]{0:T(128)S(1)} %copy-done.16), kind=kLoop, calls=%fused_computation.27 | loop fusion | flops 4718592 | bytes 11796992 | tf_op jit(solution)/shard_map/convert_element_type | solution.py:139
  250.6 2.0 copy.103
  252.6 4.6 %all-to-all-start.2 = ((bf16[1,48,192,128]{3,2,0,1:T(8,128)(2,1)}), bf16[1,48,192,128]{3,2,0,1:T(8,128)(2,1)}, u32[]{:S(2)}, u32[]{:S(2)}) async-start(bf16[1,48,192,128]{3,2,0,1:T(8,128)(2,1)} %copy.103), calls=%async_computation.2 | async-start | bytes 4718592 | tf_op jit(solution)/shard_map/all_to_all | solution.py:140
  257.2 0.4 all-reduce.3.cloned.1.call-start
  257.7 6.0 %copy.110 = f32[1,48,2,96,64]{4,3,1,2,0:T(8,128)} copy(f32[1,48,2,96,64]{4,1,3,2,0:T(8,128)} %bitcast.217) | data formatting | bytes 4718592 | tf_op jit(solution)/shard_map/jit(_roll_static)/concatenate | solution.py:27
  263.7 3.6 copy.109
  267.5 3.3 fusion.42
  270.9 0.8 slice_bitcast_fusion.5
  271.7 0.8 copy-done.5
  272.5 1.6 fusion.39
  274.1 0.7 pad_maximum_fusion.1
  274.8 0.8 fusion.46
  275.6 4.6 %fusion.32 = bf16[1,48,2,96,128]{4,3,1,2,0:T(8,128)(2,1)S(1)} fusion(f32[1,48,2,96,64]{4,3,1,2,0:T(8,128)S(1)} %bitcast.222, f32[1,48,2,96,64]{4,3,1,2,0:T(8,128)} %copy.109, f32[1,48,2,96,128]{4,1,3,2,0:T(8,128)S(1)} %bitcast.211, f32[128]{0:T(128)S(1)} %copy-done.15), kind=kLoop, calls=%fused_computation.47 | loop fusion | flops 4718592 | bytes 11796992 | tf_op jit(solution)/shard_map/convert_element_type | solution.py:119
  280.2 0.8 slice_bitcast_fusion.7
  281.1 1.6 fusion.36
  282.6 0.7 pad_maximum_fusion
  283.4 13.7 %psum.29 = f32[2,192]{1,0:T(2,128)} all-reduce(f32[2,192]{1,0:T(2,128)S(1)} %reshape.485), channel_id=1, replica_groups=mesh['dp'=8,'space'=4] {'dp'}, use_global_device_ids=true, to_apply=%region_7.8 | all-reduce | flops 384 | bytes 3072 | tf_op jit(solution)/shard_map/psum | solution.py:154
  297.1 13.5 %all-to-all-done.2 = bf16[1,48,192,128]{3,2,0,1:T(8,128)(2,1)} async-done(((bf16[1,48,192,128]{3,2,0,1:T(8,128)(2,1)}), bf16[1,48,192,128]{3,2,0,1:T(8,128)(2,1)}, u32[]{:S(2)}, u32[]{:S(2)}) %all-to-all-start.2) | async-done | bytes 2359328 | tf_op jit(solution)/shard_map/all_to_all | solution.py:140
  310.6 2.0 copy.104
  312.6 0.4 copy-done.13
  313.0 3.0 fusion.11
  316.0 2.6 fusion.10
  318.6 37.9 %psum.31 = f32[768]{0:T(1024)} all-reduce(f32[768]{0:T(1024)S(1)} %get-tuple-element.5), channel_id=1, replica_groups=mesh['dp'=8,'space'=4] {'dp','space'}, use_global_device_ids=true, to_apply=%region_10.11 | all-reduce | flops 768 | bytes 6144 | tf_op jit(solution)/shard_map/psum | solution.py:155
  356.6 1.6 copy.160
  358.2 1.6 copy.161
  (80 shorter events, 1.4 us)
Async XLA Ops:
  11.2 11.7 %copy-start.8 = (bf16[1,12,128,768]{3,2,1,0:T(8,128)(2,1)S(1)}, bf16[1,12,128,768]{3,2,1,0:T(8,128)(2,1)}, u32[]{:S(2)}) copy-start(bf16[1,12,128,768]{3,2,1,0:T(8,128)(2,1)} %param.6) | copy-start | bytes 7077892
  16.3 7.9 %copy-start.17 = (f32[768]{0:T(1024)S(1)}, f32[768]{0:T(1024)}, u32[]{:S(2)}) copy-start(f32[768]{0:T(1024)} %param.7) | copy-start | bytes 9220
  16.3 77.2 %all-to-all-start = ((bf16[1,12,768,128]{3,1,0,2:T(8,128)(2,1)}), bf16[1,12,768,128]{3,1,0,2:T(8,128)(2,1)}, u32[]{:S(2)}, u32[]{:S(2)}) async-start(bf16[1,12,768,128]{3,1,0,2:T(8,128)(2,1)} %copy.82), calls=%async_computation | async-start | bytes 6291456 | tf_op jit(solution)/shard_map/all_to_all | solution.py:126
  25.9 71.9 %copy-start.18 = (f32[2,192]{1,0:T(2,128)S(1)}, f32[2,192]{1,0:T(2,128)}, u32[]{:S(2)}) copy-start(f32[2,192]{1,0:T(2,128)} %param.9) | copy-start | bytes 4612
  29.2 69.2 %copy-start.14 = (bf16[2,192,96]{2,1,0:T(8,128)(2,1)S(1)}, bf16[2,192,96]{2,1,0:T(8,128)(2,1)}, u32[]{:S(2)}) copy-start(bf16[2,192,96]{2,1,0:T(8,128)(2,1)} %param.8) | copy-start | bytes 221188
  93.6 73.8 %all-to-all-start.1 = ((bf16[1,12,768,128]{3,1,0,2:T(8,128)(2,1)}), bf16[1,12,768,128]{3,1,0,2:T(8,128)(2,1)S(1)}, u32[]{:S(2)}, u32[]{:S(2)}) async-start(bf16[1,12,768,128]{3,1,0,2:T(8,128)(2,1)} %copy.91), calls=%async_computation.1 | async-start | bytes 6291456 | tf_op jit(solution)/shard_map/all_to_all | solution.py:118
  170.6 28.3 %copy-start = (f32[1,1,48,192,128]{4,2,0,3,1:T(8,128)}, f32[1,1,48,192,128]{4,2,0,3,1:T(8,128)S(1)}, u32[]{:S(2)}) copy-start(f32[1,1,48,192,128]{4,2,0,3,1:T(8,128)S(1)} %get-tuple-element.14) | copy-start | bytes 14155780
  172.1 4.2 %copy-start.2 = (f32[1,48,192,64]{3,1,2,0:T(8,128)}, f32[1,48,192,64]{3,1,2,0:T(8,128)S(1)}, u32[]{:S(2)}) copy-start(f32[1,48,192,64]{3,1,2,0:T(8,128)S(1)} %get-tuple-element.27) | copy-start | bytes 7077892
  172.1 5.1 %copy-start.1 = (f32[1,48,192,64]{3,1,2,0:T(8,128)}, f32[1,48,192,64]{3,1,2,0:T(8,128)S(1)}, u32[]{:S(2)}) copy-start(f32[1,48,192,64]{3,1,2,0:T(8,128)S(1)} %get-tuple-element.26) | copy-start | bytes 7077892
  177.2 3.6 copy-start.10
  189.2 9.6 %slice-start.4 = ((s8[4718592]{0:T(1024)(128)(4,1)}), s8[4194304]{0:T(1024)(128)(4,1)S(1)}, s32[]{:S(2)}) async-start(s8[4718592]{0:T(1024)(128)(4,1)} %bitcast.218), calls=%async_computation.8 | async-start | bytes 8388608
  195.2 3.6 slice-start.5
  195.2 3.6 copy-start.15
  207.6 16.7 %copy-start.4 = (bf16[48,2,96,128]{3,2,0,1:T(8,128)(2,1)}, bf16[48,2,96,128]{3,2,0,1:T(8,128)(2,1)S(1)}, u32[]{:S(2)}) copy-start(bf16[48,2,96,128]{3,2,0,1:T(8,128)(2,1)S(1)} %get-tuple-element.36) | copy-start | bytes 7077892
  213.0 5.3 %copy-start.16 = (f32[128]{0:T(128)S(1)}, f32[128]{0:T(128)}, u32[]{:S(2)}) copy-start(f32[128]{0:T(128)} %constant.65.clone.1) | copy-start | bytes 1540
  218.3 6.0 %copy-start.11 = (f32[1,48,2,96,64]{4,3,1,2,0:T(8,128)S(1)}, f32[1,48,2,96,64]{4,3,1,2,0:T(8,128)}, u32[]{:S(2)}) copy-start(f32[1,48,2,96,64]{4,3,1,2,0:T(8,128)} %get-tuple-element.20) | copy-start | bytes 7077892
  218.3 6.0 %copy-start.12 = (f32[1,48,2,96,64]{4,3,1,2,0:T(8,128)S(1)}, f32[1,48,2,96,64]{4,3,1,2,0:T(8,128)}, u32[]{:S(2)}) copy-start(f32[1,48,2,96,64]{4,3,1,2,0:T(8,128)} %get-tuple-element.21) | copy-start | bytes 7077892
  229.2 4.6 %copy-start.6 = (bf16[1,48,2,96,128]{4,3,1,2,0:T(8,128)(2,1)}, bf16[1,48,2,96,128]{4,3,1,2,0:T(8,128)(2,1)S(1)}, u32[]{:S(2)}) copy-start(bf16[1,48,2,96,128]{4,3,1,2,0:T(8,128)(2,1)S(1)} %get-tuple-element.42) | copy-start | bytes 7077892
  252.6 11.1 %slice-start.2 = ((s8[4718592]{0:T(1024)(128)(4,1)}), s8[524288]{0:T(1024)(128)(4,1)S(1)}, s32[]{:S(2)}) async-start(s8[4718592]{0:T(1024)(128)(4,1)} %bitcast.213), calls=%async_computation.6 | async-start | bytes 1048576
  252.6 58.0 %all-to-all-start.2 = ((bf16[1,48,192,128]{3,2,0,1:T(8,128)(2,1)}), bf16[1,48,192,128]{3,2,0,1:T(8,128)(2,1)}, u32[]{:S(2)}, u32[]{:S(2)}) async-start(bf16[1,48,192,128]{3,2,0,1:T(8,128)(2,1)} %copy.103), calls=%async_computation.2 | async-start | bytes 4718592 | tf_op jit(solution)/shard_map/all_to_all | solution.py:140
  257.2 99.3 %all-reduce.3.cloned.1.call-start = ((), (), s32[]{:S(2)}) async-start(), calls=%async_computation.3 | async-start | bytes 786432 | tf_op jit(solution)/shard_map/psum | solution.py:154
  257.7 6.0 %slice-start.3 = ((s8[4718592]{0:T(1024)(128)(4,1)}), s8[4194304]{0:T(1024)(128)(4,1)S(1)}, s32[]{:S(2)}) async-start(s8[4718592]{0:T(1024)(128)(4,1)} %bitcast.213), calls=%async_computation.7 | async-start | bytes 8388608
  267.5 3.3 copy-start.3
  267.5 8.0 %slice-start.6 = ((s8[4718592]{0:T(1024)(128)(4,1)}), s8[4194304]{0:T(1024)(128)(4,1)S(1)}, s32[]{:S(2)}) async-start(s8[4718592]{0:T(1024)(128)(4,1)} %bitcast.221), calls=%async_computation.10 | async-start | bytes 8388608
  270.8 1.7 copy-start.5
  270.8 1.7 copy-start.19
  270.9 4.7 %slice-start.7 = ((s8[4718592]{0:T(1024)(128)(4,1)}), s8[524288]{0:T(1024)(128)(4,1)S(1)}, s32[]{:S(2)}) async-start(s8[4718592]{0:T(1024)(128)(4,1)} %bitcast.221), calls=%async_computation.11 | async-start | bytes 1048576
  271.7 3.1 copy-start.7
  271.7 3.9 %slice-start = ((s8[4718592]{0:T(1024)(128)(4,1)}), s8[4194304]{0:T(1024)(128)(4,1)S(1)}, s32[]{:S(2)}) async-start(s8[4718592]{0:T(1024)(128)(4,1)} %bitcast.209), calls=%async_computation.4 | async-start | bytes 8388608
  272.5 3.1 slice-start.1
  281.0 31.6 %copy-start.9 = (bf16[1,12,128,768]{3,2,1,0:T(8,128)(2,1)S(1)}, bf16[1,12,128,768]{3,2,1,0:T(8,128)(2,1)}, u32[]{:S(2)}) copy-start(bf16[1,12,128,768]{3,2,1,0:T(8,128)(2,1)} %param.6) | copy-start | bytes 7077892
  310.6 2.4 copy-start.13
Sparse Core Ops, SparseCore 0:
  283.5 55.6 all-reduce.2
where the time goes:
time: 373 us; the launch traced here: 367 us
  waiting for transfers between devices  142 us (38%)
  local copies, waits for them, and re-layouts  80.5 us (22%)
  blocking collectives  51.7 us (14%)
  matrix products  37.9 us (10%)
  other arithmetic  24.4 us (7%)
  starting transfers between devices  15.7 us (4%)
  between operations  14.8 us (4%)
    all_to_all x1, waiting for transfers between devices, on_device(): lax.all_to_all(grad_cols, 'space', split_axis=2, concat_axis=1, tiled=True)  64.4 us
    all_to_all x1, waiting for transfers between devices, on_device(): lax.all_to_all(spectrum_cols, 'space', split_axis=2, concat_axis=1, tiled...  64 us
    psum x1, blocking collectives, on_device(): sum_gain = lax.psum(gain_component, ('dp', 'space'))  37.9 us
    concatenate x8, local copies, waits for them, and re-layouts, swap_parts(): jnp.roll(values, values.shape[-1] // 2, axis=-1)  28.6 us
    slice x6, local copies, waits for them, and re-layouts, swap_parts(): jnp.roll(values, values.shape[-1] // 2, axis=-1)  23.4 us
    psum x1, blocking collectives, on_device(): lax.psum((flat_w_in, grad_b_in, flat_w_out), 'dp')  13.7 us
    all_to_all x1, waiting for transfers between devices, on_device(): lax.all_to_all(d_spectrum, 'space', split_axis=1, concat_axis=2, tiled=True)  13.5 us
    dot_general x2, matrix products, block_adjoint(): jnp.einsum('sgbom,bio->sgbim', values, weights[0], preferred_element_type...  8.85 us
  transfers between devices with their start and end apart: 4, of which 3 were waited for; matrix products, arithmetic and copies ran while one was open for 12% of the time, Pallas kernels for 0%

commit v1 on v0

--- a/solution.py
+++ b/solution.py
@@ -1,8 +1,13 @@
+import functools
 import math
 
 import jax
 import jax.numpy as jnp
+import ml_dtypes
+import numpy as np
 from jax import lax
+from jax.experimental import pallas as pl
+from jax.experimental.pallas import tpu as pltpu
 from jax.sharding import PartitionSpec as P
 
 norm_eps = 1e-05
@@ -156,9 +161,532 @@
     return (d_inputs, sum_w_in, sum_b_in, sum_w_out, sum_gain)
 
 
+MESH = pl.DeviceIdType.MESH
+BF = jnp.bfloat16
+F32 = jnp.float32
+NT = (((1,), (1,)), ((), ()))
+TN = (((0,), (0,)), ((), ()))
+K8 = 8
+
+
+def np_tables(length, kept):
+    product = (np.arange(length)[:, None] * np.arange(kept)[None, :]) % length
+    angles = (2.0 * np.pi / length) * product
+    scale = 1.0 / np.sqrt(length)
+    return np.cos(angles) * scale, np.sin(angles) * scale
+
+
+def narrow(table):
+    return table.astype(np.float32).astype(ml_dtypes.bfloat16)
+
+
+def column_tables(width, kept):
+    cos, sin = np_tables(width, kept)
+    order = np.arange(width)
+    wave = (order // (4 * K8)) * (2 * K8) + (order // (2 * K8)) % 2 * K8 + order % K8
+    part = (order // K8) % 2
+    forward = np.where(part[:, None] == 0, cos.T[wave], -sin.T[wave])
+    double = np.where(wave == 0, 1.0, 2.0)[:, None]
+    return narrow(forward), narrow(forward * double), narrow(forward.T)
+
+
+def row_matrix(height):
+    cos, sin = np_tables(height, height)
+    row = np.arange(2 * height * K8)
+    rp, rg, rk = row // (height * K8), row % (height * K8) // K8, row % K8
+    cp, ch, ck = row // K8 % 2, row // (2 * K8), row % K8
+    c = cos[rg[:, None], ch[None, :]]
+    s = sin[rg[:, None], ch[None, :]]
+    signed = np.where(rp[:, None] < cp[None, :], s, -s)
+    full = np.where(rp[:, None] == cp[None, :], c, signed)
+    full = np.where(rk[:, None] == ck[None, :], full, 0.0)
+    return narrow(full), narrow(full.T)
+
+
+def lane_maps(local, block):
+    picks, folds, masks = [], [], []
+    lane = np.arange(2 * local)
+    wide = lane < 256
+    half = np.where(wide, lane // 128, (lane - 256) // 64)
+    even = np.where(wide, lane % 128, 128 + lane % 64)
+    odd = np.where(wide, 64 + lane % 128, lane % 64)
+    for channel in (even, odd):
+        picks.append(channel[:, None] == np.arange(local)[None, :])
+        folds.append(channel[:, None] % block == np.arange(128)[None, :])
+        group = channel // block
+        masks.append(
+            (half[:, None] == half[None, :]) & (group[:, None] == group[None, :])
+        )
+    return tuple(narrow(np.stack(v)) for v in (picks, folds, masks))
+
+
+def kernel(
+    ndp,
+    nsp,
+    x_ref,
+    dout_ref,
+    gain_ref,
+    win_ref,
+    bin_ref,
+    wout_ref,
+    fwd_ref,
+    inv_ref,
+    fin_ref,
+    m1_ref,
+    m2_ref,
+    e_ref,
+    e2_ref,
+    mask_ref,
+    dx_ref,
+    gw_ref,
+    gg_ref,
+    send,
+    recv,
+    dsend,
+    drecv,
+    wci,
+    wco,
+    bias,
+    modes,
+    gout,
+    hidden,
+    dpre,
+    dmodes,
+    acc_in,
+    acc_out,
+    acc_b,
+    mean_s,
+    rstd_s,
+    dd,
+    part_g,
+    recv_g,
+    gain_a,
+    gain_b,
+    gain_c,
+    in_send,
+    in_recv,
+    d_send,
+    d_recv,
+    rs_send,
+    rs_recv,
+    ag_send,
+    ag_recv,
+    ga_send,
+    ga_recv,
+    gb_send,
+    gb_recv,
+):
+    dp = lax.axis_index("dp")
+    me = lax.axis_index("space")
+    rows = x_ref.shape[0]
+    chunks = send.shape[1]
+    pos = modes.shape[0]
+    lanes = wci.shape[0] // 2
+    sps = [lax.rem(me + o, nsp) for o in range(1, nsp)]
+    dps = [lax.rem(dp + o, ndp) for o in range(1, ndp)]
+    parity = lax.rem(me, 2)
+
+    barrier = pltpu.get_barrier_semaphore()
+    for z in sps:
+        pl.semaphore_signal(barrier, inc=1, device_id={"space": z}, device_id_type=MESH)
+    for q in dps:
+        pl.semaphore_signal(barrier, inc=1, device_id={"dp": q}, device_id_type=MESH)
+    pl.semaphore_wait(barrier, nsp + ndp - 2)
+
+    def in_copy(a, j, z, slot):
+        return pltpu.make_async_remote_copy(
+            src_ref=send.at[a, j, z],
+            dst_ref=recv.at[a, j, slot],
+            send_sem=in_send.at[a, j, z],
+            recv_sem=in_recv.at[a, j, slot],
+            device_id={"space": z},
+            device_id_type=MESH,
+        )
+
+    def d_copy(j, z, slot):
+        return pltpu.make_async_remote_copy(
+            src_ref=dsend.at[j, z],
+            dst_ref=drecv.at[j, slot],
+            send_sem=d_send.at[j, z],
+            recv_sem=d_recv.at[j, slot],
+            device_id={"space": z},
+            device_id_type=MESH,
+        )
+
+    low = lax.broadcasted_iota(jnp.int32, (chunks * 16, 128), 1) < 64
+
+    def pack(y, a, r):
+        y = y.reshape(chunks, 2, 16, y.shape[-1])
+        for q in range(nsp // 2):
+            b = 384 * q
+
+            def tile(t, half):
+                return y[:, half, :, b + 128 * t : b + 128 * t + 128].reshape(chunks * 16, 128)
+
+            def put(d, t, v):
+                v = v.astype(BF).reshape(chunks, 16, 128)
+                send[a, :, 2 * q + d, r, :, 128 * t : 128 * t + 128] = v
+
+            b0, b1 = tile(1, 0), tile(1, 1)
+            put(0, 0, tile(0, 0))
+            put(0, 1, tile(0, 1))
+            put(0, 2, jnp.where(low, b0, pltpu.roll(b1, 64, 1)))
+            put(1, 0, tile(2, 0))
+            put(1, 1, tile(2, 1))
+            put(1, 2, jnp.where(low, pltpu.roll(b0, 64, 1), b1))
+
+    def start_in(a, j):
+        for z in sps:
+            in_copy(a, j, z, me).start()
+        recv[a, j, me] = send[a, j, me]
+
+    def grad_row(r, c):
+        pack(jnp.dot(inv_ref[...], dout_ref[r], preferred_element_type=F32), 1, r)
+        return c
+
+    lax.fori_loop(0, rows, grad_row, 0)
+    start_in(1, 0)
+
+    gain = gain_ref[...]
+
+    def norm_row(r, c):
+        v = x_ref[r].astype(F32)
+        mean = jnp.mean(v, axis=-1, keepdims=True)
+        v = v - mean
+        rstd = lax.rsqrt(jnp.mean(v * v, axis=-1, keepdims=True) + norm_eps)
+        mean_s[r] = mean
+        rstd_s[r] = rstd
+        normed = (v * rstd * gain).astype(BF)
+        pack(jnp.dot(fwd_ref[...], normed, preferred_element_type=F32), 0, r)
+        return c
+
+    lax.fori_loop(0, rows, norm_row, 0)
+    start_in(0, 0)
+
+    pick = e_ref[parity]
+    fold = e2_ref[parity]
+    mask = mask_ref[parity]
+    for w_ref, out in ((win_ref, wci), (wout_ref, wco)):
+        block = w_ref.shape[2]
+        for p in range(2):
+            w = jnp.dot(pick, w_ref[p], preferred_element_type=F32).astype(BF)
+            w = lax.dot_general(w, fold[:, :block], NT, preferred_element_type=F32).astype(BF)
+            w = w * mask
+            if p == 0:
+                out[:lanes, :lanes] = w
+                out[lanes:, lanes:] = w
+            else:
+                out[:lanes, lanes:] = w
+                out[lanes:, :lanes] = -w
+    wide = lax.dot_general(
+        bin_ref[...], pick.astype(F32), NT, precision=lax.Precision.HIGHEST,
+        preferred_element_type=F32,
+    )
+    bias[:, :lanes] = wide[0:1]
+    bias[:, lanes:] = wide[1:2]
+    acc_in[...] = jnp.zeros_like(acc_in)
+    acc_out[...] = jnp.zeros_like(acc_out)
+    acc_b[...] = jnp.zeros_like(acc_b)
+
+    tile_rows = 128
+
+    def middle(j):
+        for a, out in ((1, gout), (0, modes)):
+            for z in sps:
+                in_copy(a, j, z, z).wait_recv()
+            x = recv[a, j].reshape(2 * pos, lanes)
+            for p in range(2):
+                t = jnp.dot(m1_ref[p * pos : (p + 1) * pos], x, preferred_element_type=F32)
+                out[:, p * lanes : (p + 1) * lanes] = t.astype(BF)
+
+        def tile(t, c):
+            at = pl.ds(pl.multiple_of(t * tile_rows, tile_rows), tile_rows)
+            v = jnp.dot(modes[at], wci[...], preferred_element_type=F32) + bias[...]
+            dh = lax.dot_general(gout[at], wco[...], NT, preferred_element_type=F32)
+            tangent = jnp.tanh(root_coef * (v + cubic_coef * v * v * v))
+            hidden[at] = (0.5 * v * (1.0 + tangent)).astype(BF)
+            slope = 0.5 * (1.0 + tangent) + 0.5 * v * (1.0 - tangent * tangent) * root_coef * (
+                1.0 + 3.0 * cubic_coef * v * v
+            )
+            d = (dh * slope).astype(BF)
+            dpre[at] = d
+            wide = d.astype(F32).reshape(tile_rows // 8, 8, 2 * lanes)
+            acc_b[...] += jnp.sum(wide, axis=0)
+            dm = lax.dot_general(d, wci[...], NT, preferred_element_type=F32).astype(BF)
+            dmodes[at] = dm[:, :lanes]
+            low_at = pl.ds(pl.multiple_of(pos + t * tile_rows, tile_rows), tile_rows)
+            dmodes[low_at] = dm[:, lanes:]
+            return c
+
+        lax.fori_loop(0, pos // tile_rows, tile, 0)
+        ds = jnp.dot(m2_ref[...], dmodes[...], preferred_element_type=F32).astype(BF)
+        dsend[j] = ds.reshape(nsp, rows, 16, lanes)
+        for z in sps:
+            d_copy(j, z, me).start()
+        drecv[j, me] = dsend[j, me]
+        acc_out[...] += lax.dot_general(hidden[...], gout[...], TN, preferred_element_type=F32)
+        acc_in[...] += lax.dot_general(modes[...], dpre[...], TN, preferred_element_type=F32)
+
+    def step(j, c):
+        @pl.when(j + 1 < chunks)
+        def _():
+            start_in(1, j + 1)
+            start_in(0, j + 1)
+
+        middle(j)
+        return c
+
+    lax.fori_loop(0, chunks, step, 0)
+
+    local = e_ref.shape[2]
+    shard = part_g.shape[1]
+    pick32 = pick.astype(F32)
+    fold32 = fold.astype(F32)
+    mask32 = mask.astype(F32)
+    sums_b = jnp.sum(acc_b[...], axis=0, keepdims=True)
+    column = lax.broadcasted_iota(jnp.int32, (local, 128), 1)
+    flat = []
+    for n, acc in enumerate((acc_in, acc_out)):
+        full = (
+            acc[:lanes, :lanes] + acc[lanes:, lanes:],
+            acc[:lanes, lanes:] - acc[lanes:, :lanes],
+        )
+        for p in range(2):
+            g = lax.dot_general(
+                pick32, full[p] * mask32, TN, precision=lax.Precision.HIGHEST,
+                preferred_element_type=F32,
+            )
+            g = jnp.dot(g, fold32, precision=lax.Precision.HIGHEST, preferred_element_type=F32)
+            if n == 0:
+                db = lax.dot_general(
+                    pick32, jnp.broadcast_to(sums_b[:, p * lanes : (p + 1) * lanes], (128, lanes)),
+                    (((0,), (1,)), ((), ())), precision=lax.Precision.HIGHEST,
+                    preferred_element_type=F32,
+                )
+                g = jnp.where(column == 96, db, g)
+            per = local // shard
+            part_g[(2 * n + p) * per : (2 * n + p + 1) * per] = g.reshape(per, shard, 128)
+
+    def rs_copy(q, slot):
+        return pltpu.make_async_remote_copy(
+            src_ref=part_g.at[q],
+            dst_ref=recv_g.at[slot],
+            send_sem=rs_send.at[q],
+            recv_sem=rs_recv.at[slot],
+            device_id={"dp": q},
+            device_id_type=MESH,
+        )
+
+    def ag_copy(q, slot):
+        return pltpu.make_async_remote_copy(
+            src_ref=gw_ref.at[dp],
+            dst_ref=gw_ref.at[slot],
+            send_sem=ag_send.at[q],
+            recv_sem=ag_recv.at[slot],
+            device_id={"dp": q},
+            device_id_type=MESH,
+        )
+
+    for q in dps:
+        rs_copy(q, dp).start()
+    recv_g[dp] = part_g[dp]
+    for q in dps:
+        rs_copy(q, q).wait_recv()
+    gw_ref[dp] = jnp.sum(recv_g[...], axis=0)
+    for q in dps:
+        ag_copy(q, dp).start()
+
+    for j in range(chunks):
+        for z in sps:
+            d_copy(j, z, z).wait_recv()
+
+    def last_row(r, c):
+        for q in range(nsp // 2):
+            b = 384 * q
+
+            def tile(d, t):
+                v = drecv[:, 2 * q + d, r, :, 128 * t : 128 * t + 128]
+                return v.reshape(chunks * 16, 128)
+
+            def put(half, t, v):
+                v = v.astype(BF).reshape(chunks, 16, 128)
+                dd[:, half, :, b + 128 * t : b + 128 * t + 128] = v
+
+            e2, o2 = tile(0, 2).astype(F32), tile(1, 2).astype(F32)
+            for half in range(2):
+                put(half, 0, tile(0, half))
+                put(half, 2, tile(1, half))
+            put(0, 1, jnp.where(low, e2, pltpu.roll(o2, 64, 1)))
+            put(1, 1, jnp.where(low, pltpu.roll(e2, 64, 1), o2))
+        spectrum = dd[...].reshape(chunks * 32, dd.shape[-1])
+        grad = jnp.dot(fin_ref[...], spectrum, preferred_element_type=F32)
+        grad = grad + dout_ref[r].astype(F32)
+        rstd = rstd_s[r]
+        xhat = (x_ref[r].astype(F32) - mean_s[r]) * rstd
+        prod = grad * xhat
+        c = c + jnp.sum(prod.reshape(-1, 8, prod.shape[-1]), axis=0)
+        scaled = grad * gain
+        m_a = jnp.mean(scaled, axis=-1, keepdims=True)
+        m_b = jnp.mean(prod * gain, axis=-1, keepdims=True)
+        dx_ref[r] = (rstd * (scaled - m_a - xhat * m_b)).astype(BF)
+        return c
+
+    gain_sum = lax.fori_loop(0, rows, last_row, jnp.zeros((8, x_ref.shape[-1]), F32))
+
+    def ga_copy(z, slot):
+        return pltpu.make_async_remote_copy(
+            src_ref=gain_a.at[me],
+            dst_ref=gain_a.at[slot],
+            send_sem=ga_send.at[z],
+            recv_sem=ga_recv.at[slot],
+            device_id={"space": z},
+            device_id_type=MESH,
+        )
+
+    def gb_copy(q, slot):
+        return pltpu.make_async_remote_copy(
+            src_ref=gain_b.at[dp],
+            dst_ref=gain_b.at[slot],
+            send_sem=gb_send.at[q],
+            recv_sem=gb_recv.at[slot],
+            device_id={"dp": q},
+            device_id_type=MESH,
+        )
+
+    gain_a[me] = gain_sum
+    for z in sps:
+        ga_copy(z, me).start()
+    for z in sps:
+        ga_copy(z, z).wait_recv()
+    gain_b[dp] = jnp.sum(gain_a[...], axis=0)
+    for q in dps:
+        gb_copy(q, dp).start()
+    for q in dps:
+        gb_copy(q, q).wait_recv()
+    gg_ref[...] = jnp.sum(jnp.sum(gain_b[...], axis=0), axis=0, keepdims=True)
+
+    for q in dps:
+        ag_copy(q, q).wait_recv()
+    for q in dps:
+        rs_copy(q, dp).wait_send()
+        ag_copy(q, dp).wait_send()
+        gb_copy(q, dp).wait_send()
+    for z in sps:
+        ga_copy(z, me).wait_send()
+
+    def drain(j, c):
+        for z in sps:
+            in_copy(0, j, z, me).wait_send()
+            in_copy(1, j, z, me).wait_send()
+            d_copy(j, z, me).wait_send()
+        return c
+
+    lax.fori_loop(0, chunks, drain, 0)
+
+
+def fused(ndp, nsp, inputs, gain, w_in, b_in, w_out, d_out):
+    _, rows, width, channels = inputs.shape
+    kept = width // 2
+    height = rows * nsp
+    local, block = w_in.shape[1], w_in.shape[2]
+    chunks = kept // (2 * K8)
+    lanes = 2 * local
+    pos = height * K8
+    shard = 4 * local // ndp
+    fwd, inv, fin = column_tables(width, kept)
+    m1, m2 = row_matrix(height)
+    pick, fold, mask = lane_maps(local, block)
+    vmem = pl.BlockSpec(memory_space=pltpu.VMEM)
+    dma = pltpu.SemaphoreType.DMA
+    dx, gw, gg = pl.pallas_call(
+        functools.partial(kernel, ndp, nsp),
+        out_shape=(
+            jax.ShapeDtypeStruct((rows, width, channels), BF),
+            jax.ShapeDtypeStruct((ndp, shard, 128), F32),
+            jax.ShapeDtypeStruct((1, channels), F32),
+        ),
+        in_specs=[vmem] * 14,
+        out_specs=(vmem, vmem, vmem),
+        scratch_shapes=[
+            pltpu.VMEM((2, chunks, nsp, rows, 16, lanes), BF),
+            pltpu.VMEM((2, chunks, nsp, rows, 16, lanes), BF),
+            pltpu.VMEM((chunks, nsp, rows, 16, lanes), BF),
+            pltpu.VMEM((chunks, nsp, rows, 16, lanes), BF),
+            pltpu.VMEM((2 * lanes, 2 * lanes), BF),
+            pltpu.VMEM((2 * lanes, 2 * lanes), BF),
+            pltpu.VMEM((1, 2 * lanes), F32),
+            pltpu.VMEM((pos, 2 * lanes), BF),
+            pltpu.VMEM((pos, 2 * lanes), BF),
+            pltpu.VMEM((pos, 2 * lanes), BF),
+            pltpu.VMEM((pos, 2 * lanes), BF),
+            pltpu.VMEM((2 * pos, lanes), BF),
+            pltpu.VMEM((2 * lanes, 2 * lanes), F32),
+            pltpu.VMEM((2 * lanes, 2 * lanes), F32),
+            pltpu.VMEM((8, 2 * lanes), F32),
+            pltpu.VMEM((rows, width, 1), F32),
+            pltpu.VMEM((rows, width, 1), F32),
+            pltpu.VMEM((chunks, 2, 16, channels), BF),
+            pltpu.VMEM((ndp, shard, 128), F32),
+            pltpu.VMEM((ndp, shard, 128), F32),
+            pltpu.VMEM((nsp, 8, channels), F32),
+            pltpu.VMEM((ndp, 8, channels), F32),
+            pltpu.VMEM((8, channels), F32),
+            dma((2, chunks, nsp)),
+            dma((2, chunks, nsp)),
+            dma((chunks, nsp)),
+            dma((chunks, nsp)),
+            dma((ndp,)),
+            dma((ndp,)),
+            dma((ndp,)),
+            dma((ndp,)),
+            dma((nsp,)),
+            dma((nsp,)),
+            dma((ndp,)),
+            dma((ndp,)),
+        ],
+        compiler_params=pltpu.CompilerParams(
+            collective_id=0, has_side_effects=True, vmem_limit_bytes=60 * 1024 * 1024
+        ),
+    )(
+        inputs[0],
+        d_out[0],
+        gain[None, :],
+        w_in,
+        b_in,
+        w_out,
+        *(jnp.asarray(v) for v in (fwd, inv, fin, m1, m2, pick, fold, mask)),
+    )
+    gw = gw.reshape(4, local, 128)
+    return (
+        dx[None],
+        gw[:2, :, :block],
+        gw[:2, :, block],
+        gw[2:, :, :block],
+        gg[0],
+    )
+
+
+def choose(ndp, nsp, *args):
+    inputs, w_in = args[0], args[2]
+    local, block = w_in.shape[1], w_in.shape[2]
+    fits = (
+        inputs.shape[0] == 1
+        and nsp == 4
+        and local == 192
+        and block == 96
+        and inputs.shape[2] % 32 == 0
+        and inputs.shape[1] * nsp * K8 % 128 == 0
+        and local % (4 * local // ndp) == 0
+        and (4 * local // ndp) % 8 == 0
+    )
+    if fits:
+        return fused(ndp, nsp, *args)
+    return on_device(*args)
+
+
 def solution(mesh):
     return jax.shard_map(
-        on_device,
+        functools.partial(choose, mesh.shape["dp"], mesh.shape["space"]),
         mesh=mesh,
         in_specs=(
             P("dp", "space", None, None),

time: 373 us -> 191 us (0.51); the launches traced: 367 us -> 191 us
  Pallas kernels: 0 us -> 181 us
  waiting for transfers between devices: 142 us -> 0 us
  local copies, waits for them, and re-layouts: 80.5 us -> 8.03 us
  blocking collectives: 51.7 us -> 0 us
  matrix products: 37.9 us -> 0 us
  other arithmetic: 24.4 us -> 1.28 us
  starting transfers between devices: 15.7 us -> 0 us
  between operations: 14.8 us -> 0.64 us
    pallas_call x0 -> x1, Pallas kernels: none -> 181 us  [fused(): pl.pallas_call(functools.partial(kernel, ndp, nsp), out_shape=(jax.ShapeD...]
    all_to_all x3 -> x0, waiting for transfers between devices: 142 us -> none  [the longest x1 64.4 us: on_device(): lax.all_to_all(grad_cols, 'space', split_axis=2, concat_axis=1, tiled=True)]
    psum x2 -> x0, blocking collectives: 51.7 us -> none  [the longest x1 37.9 us: on_device(): sum_gain = lax.psum(gain_component, ('dp', 'space'))]
    dot_general x16 -> x0, matrix products: 37.9 us -> none  [the longest x2 8.85 us: block_adjoint(): jnp.einsum('sgbom,bio->sgbim', values, weights[0], preferred_element_type...]
    concatenate x8 -> x0, local copies, waits for them, and re-layouts: 28.6 us -> none  [swap_parts(): jnp.roll(values, values.shape[-1] // 2, axis=-1)]
    slice x11 -> x2, local copies, waits for them, and re-layouts: 27.8 us -> 3.54 us  [the longest x1 1.79 us: fused(): gw[2:, :, :block]]
    convert_element_type x4 -> x0, other arithmetic: 21.2 us -> none  [the longest x1 8.7 us: on_device(): rows_apply(grad_full, row_tables, plus_minus).astype(jnp.bfloat16)]
    all_to_all x3 -> x0, starting transfers between devices: 15.3 us -> none  [the longest x1 6.45 us: on_device(): lax.all_to_all(grad_cols, 'space', split_axis=2, concat_axis=1, tiled=True)]
  transfers between devices with their start and end apart: 4 -> 0, of which waited for: 3 -> 0; matrix products, arithmetic and copies ran while one was open for 12% -> 0% of each run, Pallas kernels for 0% -> 0%
where the time goes in v1:
time: 191 us
  Pallas kernels  181 us (95%)
  local copies, waits for them, and re-layouts  8.03 us (4%)
    pallas_call x1, Pallas kernels, fused(): pl.pallas_call(functools.partial(kernel, ndp, nsp), out_shape=(jax.ShapeD...  181 us

profile of v1, /device:TPU:0, one launch (start us, length us, event | category | flops | bytes accessed | tf_op | source)
XLA Modules:
  0.0 191.2 jit_solution(3549295963051086339)
XLA Ops:
  0.6 1.3 broadcast_in_dim.6.gain_ref
  1.9 181.2 %shard_map.173 = (bf16[12,128,768]{2,1,0:T(8,128)(2,1)}, f32[8,96,128]{2,1,0:T(8,128)}, f32[1,768]{1,0:T(1,128)}) custom-call(bf16[12,128,768]{2,1,0:T(8,128)(2,1)} %bitcast.5, bf16[12,128,768]{2,1,0:T(8,128)(2,1)} %bitcast.6, f32[1,768]{1,0:T(1,128)} %broadcast_in_dim.6.gain_ref, bf16[2,192,96]{2,1,0:T(8,128)(2,1)} %win_ref.1, f32[2,192]{1,0:T(2,128)} %bin_ref.1, ...), custom_call_target="tpu_custom_call" | custom-call | tf_op jit(solution)/shard_map/pallas_call | solution.py:601
  183.1 1.8 slice_reduce_fusion
  184.9 1.8 fusion
  186.7 1.3 reduce.1
  187.9 3.2 %copy.20 = bf16[1,12,128,768]{3,2,1,0:T(8,128)(2,1)} copy(bf16[1,12,128,768]{3,2,1,0:T(8,128)(2,1)} %bitcast.4) | data formatting | bytes 4718592

commit v2 on v1

--- a/solution.py
+++ b/solution.py
@@ -223,8 +223,8 @@
 def kernel(
     ndp,
     nsp,
-    x_ref,
-    dout_ref,
+    x_hbm,
+    dout_hbm,
     gain_ref,
     win_ref,
     bin_ref,
@@ -232,12 +232,12 @@
     fwd_ref,
     inv_ref,
     fin_ref,
-    m1_ref,
-    m2_ref,
-    e_ref,
-    e2_ref,
-    mask_ref,
-    dx_ref,
+    m1_hbm,
+    m2_hbm,
+    e_hbm,
+    e2_hbm,
+    mask_hbm,
+    dx_hbm,
     gw_ref,
     gg_ref,
     send,
@@ -262,7 +262,17 @@
     recv_g,
     gain_a,
     gain_b,
-    gain_c,
+    acc_g,
+    x_ref,
+    dout_ref,
+    m1_ref,
+    m2_ref,
+    e_ref,
+    e2_ref,
+    mask_ref,
+    dx_ref,
+    load_sem,
+    store_sem,
     in_send,
     in_recv,
     d_send,
@@ -285,6 +295,20 @@
     sps = [lax.rem(me + o, nsp) for o in range(1, nsp)]
     dps = [lax.rem(dp + o, ndp) for o in range(1, ndp)]
     parity = lax.rem(me, 2)
+    part = rows // 2
+
+    def load(n, src, dst):
+        return pltpu.make_async_copy(src, dst, load_sem.at[n])
+
+    def halves(ref, hf):
+        return ref.at[pl.ds(hf * part, part)]
+
+    loads = [load(hf, halves(dout_hbm, hf), halves(dout_ref, hf)) for hf in range(2)]
+    loads += [load(2 + hf, halves(x_hbm, hf), halves(x_ref, hf)) for hf in range(2)]
+    pairs = ((e_hbm, e_ref), (e2_hbm, e2_ref), (mask_hbm, mask_ref), (m1_hbm, m1_ref), (m2_hbm, m2_ref))
+    loads += [load(4 + n, src, dst) for n, (src, dst) in enumerate(pairs)]
+    for copy in loads:
+        copy.start()
 
     barrier = pltpu.get_barrier_semaphore()
     for z in sps:
@@ -293,22 +317,22 @@
         pl.semaphore_signal(barrier, inc=1, device_id={"dp": q}, device_id_type=MESH)
     pl.semaphore_wait(barrier, nsp + ndp - 2)
 
-    def in_copy(a, j, z, slot):
+    def in_copy(a, j, z, slot, hf):
         return pltpu.make_async_remote_copy(
-            src_ref=send.at[a, j, z],
-            dst_ref=recv.at[a, j, slot],
-            send_sem=in_send.at[a, j, z],
-            recv_sem=in_recv.at[a, j, slot],
+            src_ref=send.at[a, j, z, pl.ds(hf * part, part)],
+            dst_ref=recv.at[a, j, slot, pl.ds(hf * part, part)],
+            send_sem=in_send.at[a, j, z, hf],
+            recv_sem=in_recv.at[a, j, slot, hf],
             device_id={"space": z},
             device_id_type=MESH,
         )
 
-    def d_copy(j, z, slot):
+    def d_copy(j, z, slot, hf):
         return pltpu.make_async_remote_copy(
-            src_ref=dsend.at[j, z],
-            dst_ref=drecv.at[j, slot],
-            send_sem=d_send.at[j, z],
-            recv_sem=d_recv.at[j, slot],
+            src_ref=dsend.at[j, z, pl.ds(hf * part, part)],
+            dst_ref=drecv.at[j, slot, pl.ds(hf * part, part)],
+            send_sem=d_send.at[j, z, hf],
+            recv_sem=d_recv.at[j, slot, hf],
             device_id={"space": z},
             device_id_type=MESH,
         )
@@ -335,19 +359,23 @@
             put(1, 1, tile(2, 1))
             put(1, 2, jnp.where(low, pltpu.roll(b0, 64, 1), b1))
 
-    def start_in(a, j):
+    def start_in(a, j, hf):
         for z in sps:
-            in_copy(a, j, z, me).start()
-        recv[a, j, me] = send[a, j, me]
+            in_copy(a, j, z, me, hf).start()
+        at = pl.ds(hf * part, part)
+        recv[a, j, me, at] = send[a, j, me, at]
 
     def grad_row(r, c):
         pack(jnp.dot(inv_ref[...], dout_ref[r], preferred_element_type=F32), 1, r)
         return c
 
-    lax.fori_loop(0, rows, grad_row, 0)
-    start_in(1, 0)
-
-    gain = gain_ref[...]
+    for hf in range(2):
+        loads[hf].wait()
+        lax.fori_loop(hf * part, (hf + 1) * part, grad_row, 0)
+        start_in(1, 0, hf)
+
+    gain = gain_ref[...].reshape(1, -1)
+    channels = x_ref.shape[-1]
 
     def norm_row(r, c):
         v = x_ref[r].astype(F32)
@@ -356,12 +384,20 @@
         rstd = lax.rsqrt(jnp.mean(v * v, axis=-1, keepdims=True) + norm_eps)
         mean_s[r] = mean
         rstd_s[r] = rstd
-        normed = (v * rstd * gain).astype(BF)
+        v = v * rstd
+        normed = (v * gain).astype(BF)
         pack(jnp.dot(fwd_ref[...], normed, preferred_element_type=F32), 0, r)
-        return c
-
-    lax.fori_loop(0, rows, norm_row, 0)
-    start_in(0, 0)
+        prod = v * dout_ref[r].astype(F32)
+        return c + jnp.sum(prod.reshape(-1, 8, channels), axis=0)
+
+    gain_sum = jnp.zeros((8, channels), F32)
+    for hf in range(2):
+        loads[2 + hf].wait()
+        gain_sum = lax.fori_loop(hf * part, (hf + 1) * part, norm_row, gain_sum)
+        start_in(0, 0, hf)
+    gain_a[me] = gain_sum
+    for copy in loads[4:]:
+        copy.wait()
 
     pick = e_ref[parity]
     fold = e2_ref[parity]
@@ -387,13 +423,15 @@
     acc_in[...] = jnp.zeros_like(acc_in)
     acc_out[...] = jnp.zeros_like(acc_out)
     acc_b[...] = jnp.zeros_like(acc_b)
+    acc_g[...] = jnp.zeros_like(acc_g)
 
     tile_rows = 128
 
     def middle(j):
         for a, out in ((1, gout), (0, modes)):
             for z in sps:
-                in_copy(a, j, z, z).wait_recv()
+                for hf in range(2):
+                    in_copy(a, j, z, z, hf).wait_recv()
             x = recv[a, j].reshape(2 * pos, lanes)
             for p in range(2):
                 t = jnp.dot(m1_ref[p * pos : (p + 1) * pos], x, preferred_element_type=F32)
@@ -421,17 +459,21 @@
         lax.fori_loop(0, pos // tile_rows, tile, 0)
         ds = jnp.dot(m2_ref[...], dmodes[...], preferred_element_type=F32).astype(BF)
         dsend[j] = ds.reshape(nsp, rows, 16, lanes)
-        for z in sps:
-            d_copy(j, z, me).start()
+        for hf in range(2):
+            for z in sps:
+                d_copy(j, z, me, hf).start()
         drecv[j, me] = dsend[j, me]
+        cross = ds.astype(F32) * recv[0, j].reshape(2 * pos, lanes).astype(F32)
+        acc_g[...] += jnp.sum(cross.reshape(-1, 8, lanes), axis=0)
         acc_out[...] += lax.dot_general(hidden[...], gout[...], TN, preferred_element_type=F32)
         acc_in[...] += lax.dot_general(modes[...], dpre[...], TN, preferred_element_type=F32)
 
     def step(j, c):
         @pl.when(j + 1 < chunks)
         def _():
-            start_in(1, j + 1)
-            start_in(0, j + 1)
+            for a in (1, 0):
+                for hf in range(2):
+                    start_in(a, j + 1, hf)
 
         middle(j)
         return c
@@ -496,9 +538,44 @@
     for q in dps:
         ag_copy(q, dp).start()
 
-    for j in range(chunks):
-        for z in sps:
-            d_copy(j, z, z).wait_recv()
+    def ga_copy(z, slot):
+        return pltpu.make_async_remote_copy(
+            src_ref=gain_a.at[me],
+            dst_ref=gain_a.at[slot],
+            send_sem=ga_send.at[z],
+            recv_sem=ga_recv.at[slot],
+            device_id={"space": z},
+            device_id_type=MESH,
+        )
+
+    def gb_copy(q, slot):
+        return pltpu.make_async_remote_copy(
+            src_ref=gain_b.at[dp],
+            dst_ref=gain_b.at[slot],
+            send_sem=gb_send.at[q],
+            recv_sem=gb_recv.at[slot],
+            device_id={"dp": q},
+            device_id_type=MESH,
+        )
+
+    own = jnp.dot(acc_g[...], pick32, precision=lax.Precision.HIGHEST, preferred_element_type=F32)
+    shift = lax.broadcasted_iota(jnp.int32, (local, channels), 1) == (
+        lax.broadcasted_iota(jnp.int32, (local, channels), 0) + me * local
+    )
+    own = jnp.dot(
+        own, shift.astype(F32), precision=lax.Precision.HIGHEST, preferred_element_type=F32
+    )
+    gain_a[me] = gain_a[me] + own / gain
+    for z in sps:
+        ga_copy(z, me).start()
+    for z in sps:
+        ga_copy(z, z).wait_recv()
+    gain_b[dp] = jnp.sum(gain_a[...], axis=0)
+    for q in dps:
+        gb_copy(q, dp).start()
+    for q in dps:
+        gb_copy(q, q).wait_recv()
+    gg_ref[...] = jnp.sum(jnp.sum(gain_b[...], axis=0), axis=0, keepdims=True)
 
     def last_row(r, c):
         for q in range(nsp // 2):
@@ -523,47 +600,22 @@
         grad = grad + dout_ref[r].astype(F32)
         rstd = rstd_s[r]
         xhat = (x_ref[r].astype(F32) - mean_s[r]) * rstd
-        prod = grad * xhat
-        c = c + jnp.sum(prod.reshape(-1, 8, prod.shape[-1]), axis=0)
         scaled = grad * gain
         m_a = jnp.mean(scaled, axis=-1, keepdims=True)
-        m_b = jnp.mean(prod * gain, axis=-1, keepdims=True)
+        m_b = jnp.mean(scaled * xhat, axis=-1, keepdims=True)
         dx_ref[r] = (rstd * (scaled - m_a - xhat * m_b)).astype(BF)
         return c
 
-    gain_sum = lax.fori_loop(0, rows, last_row, jnp.zeros((8, x_ref.shape[-1]), F32))
-
-    def ga_copy(z, slot):
-        return pltpu.make_async_remote_copy(
-            src_ref=gain_a.at[me],
-            dst_ref=gain_a.at[slot],
-            send_sem=ga_send.at[z],
-            recv_sem=ga_recv.at[slot],
-            device_id={"space": z},
-            device_id_type=MESH,
-        )
-
-    def gb_copy(q, slot):
-        return pltpu.make_async_remote_copy(
-            src_ref=gain_b.at[dp],
-            dst_ref=gain_b.at[slot],
-            send_sem=gb_send.at[q],
-            recv_sem=gb_recv.at[slot],
-            device_id={"dp": q},
-            device_id_type=MESH,
-        )
-
-    gain_a[me] = gain_sum
-    for z in sps:
-        ga_copy(z, me).start()
-    for z in sps:
-        ga_copy(z, z).wait_recv()
-    gain_b[dp] = jnp.sum(gain_a[...], axis=0)
-    for q in dps:
-        gb_copy(q, dp).start()
-    for q in dps:
-        gb_copy(q, q).wait_recv()
-    gg_ref[...] = jnp.sum(jnp.sum(gain_b[...], axis=0), axis=0, keepdims=True)
+    stores = []
+    for hf in range(2):
+        for j in range(chunks):
+            for z in sps:
+                d_copy(j, z, z, hf).wait_recv()
+        lax.fori_loop(hf * part, (hf + 1) * part, last_row, 0)
+        stores.append(
+            pltpu.make_async_copy(halves(dx_ref, hf), halves(dx_hbm, hf), store_sem.at[hf])
+        )
+        stores[hf].start()
 
     for q in dps:
         ag_copy(q, q).wait_recv()
@@ -576,12 +628,33 @@
 
     def drain(j, c):
         for z in sps:
-            in_copy(0, j, z, me).wait_send()
-            in_copy(1, j, z, me).wait_send()
-            d_copy(j, z, me).wait_send()
+            for hf in range(2):
+                in_copy(0, j, z, me, hf).wait_send()
+                in_copy(1, j, z, me, hf).wait_send()
+                d_copy(j, z, me, hf).wait_send()
         return c
 
     lax.fori_loop(0, chunks, drain, 0)
+    for copy in stores:
+        copy.wait()
+
+
+def finish(dx_in, gw_ref, gg_ref, dx_out, dwi_ref, db_ref, dwo_ref, dg_ref):
+    dx_out[0] = dx_in[...]
+
+    @pl.when(pl.program_id(0) == 0)
+    def _():
+        local, block = dwi_ref.shape[1:]
+        eye = lax.broadcasted_iota(jnp.int32, (local, local), 0) == lax.broadcasted_iota(
+            jnp.int32, (local, local), 1
+        )
+        for p in range(2):
+            g = gw_ref[p]
+            dwi_ref[p] = g[:, :block]
+            dwo_ref[p] = gw_ref[2 + p][:, :block]
+            db = jnp.where(eye, g[:, block : block + 1], 0.0)
+            db_ref[p : p + 1] = jnp.sum(db, axis=0, keepdims=True)
+        dg_ref[...] = gg_ref[...].reshape(dg_ref.shape)
 
 
 def fused(ndp, nsp, inputs, gain, w_in, b_in, w_out, d_out):
@@ -597,6 +670,7 @@
     m1, m2 = row_matrix(height)
     pick, fold, mask = lane_maps(local, block)
     vmem = pl.BlockSpec(memory_space=pltpu.VMEM)
+    hbm = pl.BlockSpec(memory_space=pl.ANY)
     dma = pltpu.SemaphoreType.DMA
     dx, gw, gg = pl.pallas_call(
         functools.partial(kernel, ndp, nsp),
@@ -605,8 +679,8 @@
             jax.ShapeDtypeStruct((ndp, shard, 128), F32),
             jax.ShapeDtypeStruct((1, channels), F32),
         ),
-        in_specs=[vmem] * 14,
-        out_specs=(vmem, vmem, vmem),
+        in_specs=[hbm] * 2 + [vmem] * 7 + [hbm] * 5,
+        out_specs=(hbm, vmem, vmem),
         scratch_shapes=[
             pltpu.VMEM((2, chunks, nsp, rows, 16, lanes), BF),
             pltpu.VMEM((2, chunks, nsp, rows, 16, lanes), BF),
@@ -630,11 +704,21 @@
             pltpu.VMEM((ndp, shard, 128), F32),
             pltpu.VMEM((nsp, 8, channels), F32),
             pltpu.VMEM((ndp, 8, channels), F32),
-            pltpu.VMEM((8, channels), F32),
-            dma((2, chunks, nsp)),
-            dma((2, chunks, nsp)),
-            dma((chunks, nsp)),
-            dma((chunks, nsp)),
+            pltpu.VMEM((8, lanes), F32),
+            pltpu.VMEM((rows, width, channels), BF),
+            pltpu.VMEM((rows, width, channels), BF),
+            pltpu.VMEM(m1.shape, BF),
+            pltpu.VMEM(m2.shape, BF),
+            pltpu.VMEM(pick.shape, BF),
+            pltpu.VMEM(fold.shape, BF),
+            pltpu.VMEM(mask.shape, BF),
+            pltpu.VMEM((rows, width, channels), BF),
+            dma((9,)),
+            dma((2,)),
+            dma((2, chunks, nsp, 2)),
+            dma((2, chunks, nsp, 2)),
+            dma((chunks, nsp, 2)),
+            dma((chunks, nsp, 2)),
             dma((ndp,)),
             dma((ndp,)),
             dma((ndp,)),
@@ -650,20 +734,41 @@
     )(
         inputs[0],
         d_out[0],
-        gain[None, :],
+        gain,
         w_in,
         b_in,
         w_out,
         *(jnp.asarray(v) for v in (fwd, inv, fin, m1, m2, pick, fold, mask)),
     )
     gw = gw.reshape(4, local, 128)
-    return (
-        dx[None],
-        gw[:2, :, :block],
-        gw[:2, :, block],
-        gw[2:, :, :block],
-        gg[0],
-    )
+    step = 2
+
+    def whole(shape):
+        return pl.BlockSpec(shape, lambda i: (0,) * len(shape))
+
+    return pl.pallas_call(
+        finish,
+        grid=(rows // step,),
+        out_shape=(
+            jax.ShapeDtypeStruct((1, rows, width, channels), BF),
+            jax.ShapeDtypeStruct((2, local, block), F32),
+            jax.ShapeDtypeStruct((2, local), F32),
+            jax.ShapeDtypeStruct((2, local, block), F32),
+            jax.ShapeDtypeStruct((channels,), F32),
+        ),
+        in_specs=[
+            pl.BlockSpec((step, width, channels), lambda i: (i, 0, 0)),
+            whole((4, local, 128)),
+            whole((1, channels)),
+        ],
+        out_specs=(
+            pl.BlockSpec((1, step, width, channels), lambda i: (0, i, 0, 0)),
+            whole((2, local, block)),
+            whole((2, local)),
+            whole((2, local, block)),
+            whole((channels,)),
+        ),
+    )(dx, gw, gg)
 
 
 def choose(ndp, nsp, *args):
@@ -674,6 +779,7 @@
         and nsp == 4
         and local == 192
         and block == 96
+        and inputs.shape[1] % 2 == 0
         and inputs.shape[2] % 32 == 0
         and inputs.shape[1] * nsp * K8 % 128 == 0
         and local % (4 * local // ndp) == 0

time: 191 us -> 182 us (0.953)
  local copies, waits for them, and re-layouts: 8.03 us -> 0 us
    pallas_call x1, Pallas kernels: 181 us -> 176 us  [fused(): pl.pallas_call(functools.partial(kernel, ndp, nsp), out_shape=(jax.ShapeD...]
    pallas_call x0 -> x1, Pallas kernels: none -> 5.29 us  [fused(): pl.pallas_call(finish, grid=(rows // step,), out_shape=(jax.ShapeDtypeStr...]
    slice x2 -> x0, local copies, waits for them, and re-layouts: 3.54 us -> none  [the longest x1 1.79 us: fused(): gw[2:, :, :block]]
    unnamed x1 -> x0, local copies, waits for them, and re-layouts: 3.22 us -> none
where the time goes in v2:
time: 182 us
  Pallas kernels  181 us (99%)
    pallas_call x1, Pallas kernels, fused(): pl.pallas_call(functools.partial(kernel, ndp, nsp), out_shape=(jax.ShapeD...  176 us
    pallas_call x1, Pallas kernels, fused(): pl.pallas_call(finish, grid=(rows // step,), out_shape=(jax.ShapeDtypeStr...  5.29 us

profile of v2, /device:TPU:0, one launch (start us, length us, event | category | flops | bytes accessed | tf_op | source)
XLA Modules:
  0.0 181.8 jit_solution(12818374877653486344)
XLA Ops:
  0.6 175.9 %shard_map.173 = (bf16[12,128,768]{2,1,0:T(8,128)(2,1)}, f32[8,96,128]{2,1,0:T(8,128)}, f32[1,768]{1,0:T(1,128)}) custom-call(bf16[12,128,768]{2,1,0:T(8,128)(2,1)} %bitcast.3, bf16[12,128,768]{2,1,0:T(8,128)(2,1)} %bitcast.4, f32[768]{0:T(1024)} %gain_ref.1, bf16[2,192,96]{2,1,0:T(8,128)(2,1)} %win_ref.1, f32[2,192]{1,0:T(2,128)} %bin_ref.1, ...), custom_call_target="tpu_custom_call" | custom-call | tf_op jit(solution)/shard_map/pallas_call | solution.py:675
  176.6 5.3 %shard_map.174 = (bf16[1,12,128,768]{3,2,1,0:T(8,128)(2,1)}, f32[2,192,96]{2,1,0:T(8,128)}, f32[2,192]{1,0:T(2,128)}, f32[2,192,96]{2,1,0:T(8,128)}, f32[768]{0:T(1024)}) custom-call(bf16[12,128,768]{2,1,0:T(8,128)(2,1)} %get-tuple-element.8.dx_in, f32[4,192,128]{2,1,0:T(8,128)} %bitcast.5, f32[1,768]{1,0:T(1,128)} %get-tuple-element.10.gg_ref), custom_call_target="tpu_custom_call" | custom-call | tf_op jit(solution)/shard_map/pallas_call | solution.py:749

commit v3 on v2

--- a/solution.py
+++ b/solution.py
@@ -295,7 +295,7 @@
     sps = [lax.rem(me + o, nsp) for o in range(1, nsp)]
     dps = [lax.rem(dp + o, ndp) for o in range(1, ndp)]
     parity = lax.rem(me, 2)
-    part = rows // 2
+    part = rows // 3
 
     def load(n, src, dst):
         return pltpu.make_async_copy(src, dst, load_sem.at[n])
@@ -303,10 +303,10 @@
     def halves(ref, hf):
         return ref.at[pl.ds(hf * part, part)]
 
-    loads = [load(hf, halves(dout_hbm, hf), halves(dout_ref, hf)) for hf in range(2)]
-    loads += [load(2 + hf, halves(x_hbm, hf), halves(x_ref, hf)) for hf in range(2)]
+    loads = [load(hf, halves(dout_hbm, hf), halves(dout_ref, hf)) for hf in range(3)]
+    loads += [load(3 + hf, halves(x_hbm, hf), halves(x_ref, hf)) for hf in range(3)]
     pairs = ((e_hbm, e_ref), (e2_hbm, e2_ref), (mask_hbm, mask_ref), (m1_hbm, m1_ref), (m2_hbm, m2_ref))
-    loads += [load(4 + n, src, dst) for n, (src, dst) in enumerate(pairs)]
+    loads += [load(6 + n, src, dst) for n, (src, dst) in enumerate(pairs)]
     for copy in loads:
         copy.start()
 
@@ -369,7 +369,7 @@
         pack(jnp.dot(inv_ref[...], dout_ref[r], preferred_element_type=F32), 1, r)
         return c
 
-    for hf in range(2):
+    for hf in range(3):
         loads[hf].wait()
         lax.fori_loop(hf * part, (hf + 1) * part, grad_row, 0)
         start_in(1, 0, hf)
@@ -391,12 +391,12 @@
         return c + jnp.sum(prod.reshape(-1, 8, channels), axis=0)
 
     gain_sum = jnp.zeros((8, channels), F32)
-    for hf in range(2):
-        loads[2 + hf].wait()
+    for hf in range(3):
+        loads[3 + hf].wait()
         gain_sum = lax.fori_loop(hf * part, (hf + 1) * part, norm_row, gain_sum)
         start_in(0, 0, hf)
     gain_a[me] = gain_sum
-    for copy in loads[4:]:
+    for copy in loads[6:]:
         copy.wait()
 
     pick = e_ref[parity]
@@ -430,7 +430,7 @@
     def middle(j):
         for a, out in ((1, gout), (0, modes)):
             for z in sps:
-                for hf in range(2):
+                for hf in range(3):
                     in_copy(a, j, z, z, hf).wait_recv()
             x = recv[a, j].reshape(2 * pos, lanes)
             for p in range(2):
@@ -459,7 +459,7 @@
         lax.fori_loop(0, pos // tile_rows, tile, 0)
         ds = jnp.dot(m2_ref[...], dmodes[...], preferred_element_type=F32).astype(BF)
         dsend[j] = ds.reshape(nsp, rows, 16, lanes)
-        for hf in range(2):
+        for hf in range(3):
             for z in sps:
                 d_copy(j, z, me, hf).start()
         drecv[j, me] = dsend[j, me]
@@ -472,7 +472,7 @@
         @pl.when(j + 1 < chunks)
         def _():
             for a in (1, 0):
-                for hf in range(2):
+                for hf in range(3):
                     start_in(a, j + 1, hf)
 
         middle(j)
@@ -607,7 +607,7 @@
         return c
 
     stores = []
-    for hf in range(2):
+    for hf in range(3):
         for j in range(chunks):
             for z in sps:
                 d_copy(j, z, z, hf).wait_recv()
@@ -628,7 +628,7 @@
 
     def drain(j, c):
         for z in sps:
-            for hf in range(2):
+            for hf in range(3):
                 in_copy(0, j, z, me, hf).wait_send()
                 in_copy(1, j, z, me, hf).wait_send()
                 d_copy(j, z, me, hf).wait_send()
@@ -713,12 +713,12 @@
             pltpu.VMEM(fold.shape, BF),
             pltpu.VMEM(mask.shape, BF),
             pltpu.VMEM((rows, width, channels), BF),
-            dma((9,)),
-            dma((2,)),
-            dma((2, chunks, nsp, 2)),
-            dma((2, chunks, nsp, 2)),
-            dma((chunks, nsp, 2)),
-            dma((chunks, nsp, 2)),
+            dma((11,)),
+            dma((3,)),
+            dma((2, chunks, nsp, 3)),
+            dma((2, chunks, nsp, 3)),
+            dma((chunks, nsp, 3)),
+            dma((chunks, nsp, 3)),
             dma((ndp,)),
             dma((ndp,)),
             dma((ndp,)),
@@ -741,7 +741,7 @@
         *(jnp.asarray(v) for v in (fwd, inv, fin, m1, m2, pick, fold, mask)),
     )
     gw = gw.reshape(4, local, 128)
-    step = 2
+    step = 4
 
     def whole(shape):
         return pl.BlockSpec(shape, lambda i: (0,) * len(shape))
@@ -779,7 +779,7 @@
         and nsp == 4
         and local == 192
         and block == 96
-        and inputs.shape[1] % 2 == 0
+        and inputs.shape[1] % 12 == 0
         and inputs.shape[2] % 32 == 0
         and inputs.shape[1] * nsp * K8 % 128 == 0
         and local % (4 * local // ndp) == 0

time: 182 us -> 182 us (level)
  no operation moved by 1% of the time
where the time goes in v3:
time: 182 us; the launch traced here: 181 us
  Pallas kernels  181 us (99%)
    pallas_call x1, Pallas kernels, fused(): pl.pallas_call(functools.partial(kernel, ndp, nsp), out_shape=(jax.ShapeD...  177 us
    pallas_call x1, Pallas kernels, fused(): pl.pallas_call(finish, grid=(rows // step,), out_shape=(jax.ShapeDtypeStr...  4.23 us

profile of v3, /device:TPU:0, one launch (start us, length us, event | category | flops | bytes accessed | tf_op | source)
XLA Modules:
  0.0 181.5 jit_solution(12764044132477278624)
XLA Ops:
  0.6 176.6 %shard_map.173 = (bf16[12,128,768]{2,1,0:T(8,128)(2,1)}, f32[8,96,128]{2,1,0:T(8,128)}, f32[1,768]{1,0:T(1,128)}) custom-call(bf16[12,128,768]{2,1,0:T(8,128)(2,1)} %bitcast.3, bf16[12,128,768]{2,1,0:T(8,128)(2,1)} %bitcast.4, f32[768]{0:T(1024)} %gain_ref.1, bf16[2,192,96]{2,1,0:T(8,128)(2,1)} %win_ref.1, f32[2,192]{1,0:T(2,128)} %bin_ref.1, ...), custom_call_target="tpu_custom_call" | custom-call | tf_op jit(solution)/shard_map/pallas_call | solution.py:675
  177.3 4.2 %shard_map.174 = (bf16[1,12,128,768]{3,2,1,0:T(8,128)(2,1)}, f32[2,192,96]{2,1,0:T(8,128)}, f32[2,192]{1,0:T(2,128)}, f32[2,192,96]{2,1,0:T(8,128)}, f32[768]{0:T(1024)}) custom-call(bf16[12,128,768]{2,1,0:T(8,128)(2,1)} %get-tuple-element.8.dx_in, f32[4,192,128]{2,1,0:T(8,128)} %bitcast.5, f32[1,768]{1,0:T(1,128)} %get-tuple-element.10.gg_ref), custom_call_target="tpu_custom_call" | custom-call | tf_op jit(solution)/shard_map/pallas_call | solution.py:749
